TPU v7x, 128 devices: a whole 4x4x4 slice. The times are simulated.
128 devices in a mesh: dp: 16 (over y_hi, z, core), tp: 8 (over y_lo, x).
Axes of the slice: x: 4, y: 4 (y_hi: 2, y_lo: 2; y = y_hi * 2 + y_lo), z: 4, core: 2. Of those that a mesh axis runs over, the one named last changes fastest.
Arguments:
- hidden: bfloat16 [2, 64, 4096], P(None, 'dp'), may hold values from -500 to 500
- lengths: int32 [64], P('dp'), may hold values from 512 to 4096, as said below
- norm_gain: float32 [4096], replicated, may hold values from 0.1 to 1.9
- w_query: bfloat16 [4096, 4096], P(None, 'tp'), may hold values from -0.09375 to 0.09375
- key_weight_matrix: bfloat16 [4096, 1024], P(None, 'tp'), may hold values from -0.1875 to 0.1875
- value_weight_matrix: bfloat16 [4096, 1024], P(None, 'tp'), may hold values from -0.09375 to 0.09375
- w_out: bfloat16 [4096, 4096], P('tp'), may hold values from -0.75 to 0.75
- key_cache: bfloat16 [64, 8, 4096, 128], P('dp', 'tp'), may hold values from -1300 to 1300
- cached_value_rows: bfloat16 [64, 8, 4096, 128], P('dp', 'tp'), may hold values from -6 to 6
- next_query: bfloat16 [4096, 4096], P(('dp', 'tp')), may hold values from -0.09375 to 0.09375
- upcoming_key_weight: bfloat16 [1024, 4096], P(('dp', 'tp')), may hold values from -0.09375 to 0.09375
- upcoming_value_weight: bfloat16 [1024, 4096], P(('dp', 'tp')), may hold values from -0.09375 to 0.09375
Outputs:
- mixed: bfloat16 [2, 64, 4096], P(None, 'dp')
- next_query_tp: bfloat16 [4096, 4096], P('tp')
- next_key_tp: bfloat16 [1024, 4096], P('tp')
- next_value_tp: bfloat16 [1024, 4096], P('tp')
Inputs may be any that keep to these rules, and one draw needn't show every extreme that they name: At least one row has all 4096 slots valid; the first lengths[r] slots of row r hold its context.
All inputs are finite; a program needn't handle non-finite values.
Results may differ from a plain program's by a relative error of at most 0.012.
The roundings to bfloat16 on the way count: a program that leaves them out, or rounds other values in their place, can miss the bound.
Values may be sent and summed in bfloat16 or wider, within the bound.
A program may use at most 192 MiB of HBM per device.

v0:
```python
import math

import jax
import jax.numpy as jnp
from jax import lax
from jax.sharding import PartitionSpec as P


def as_sent(array):

    def short(part):
        return part.astype(jnp.bfloat16) if part.dtype == jnp.float32 else part

    return jax.tree.map(short, array)


def normalize(rows_in, gain):
    values = rows_in.astype(jnp.float32)
    scale = lax.rsqrt(jnp.mean(values * values, axis=-1, keepdims=True) + 1e-06)
    return (values * scale * gain).astype(jnp.bfloat16)


def apply_rotation(vectors, token_positions):
    head_size = vectors.shape[-1]
    midpoint = head_size // 2
    frequency = jnp.power(1000000.0, -jnp.arange(midpoint, dtype=jnp.float32) * 2.0 / head_size)
    angles = token_positions.astype(jnp.float32)[:, None] * frequency[None, :]
    cosine = jnp.concatenate([jnp.cos(angles), jnp.cos(angles)], axis=-1)[:, None, :]
    sine_part = jnp.concatenate([jnp.sin(angles), jnp.sin(angles)], axis=-1)[:, None, :]
    leading = vectors[..., :midpoint]
    trailing = vectors[..., midpoint:]
    turned = jnp.concatenate([-trailing, leading], axis=-1)
    return vectors * cosine + turned * sine_part


def reshard(weights):
    gathered = (
        lax.all_gather(weights[0], "dp", axis=0, tiled=True),
        lax.all_gather(weights[1], "dp", axis=0, tiled=True),
        lax.all_gather(weights[2], "dp", axis=0, tiled=True),
    )
    dp_count = lax.axis_size("dp")
    stacked = tuple(
        (
            piece.reshape(dp_count, 1, piece.shape[0] // dp_count, piece.shape[1])
            for piece in gathered
        )
    )
    moved = jax.tree.map(
        lambda part, own: part.astype(own.dtype),
        lax.all_to_all(as_sent(stacked), "tp", split_axis=0, concat_axis=1, tiled=True),
        stacked,
    )
    return tuple((piece.reshape(-1, piece.shape[3]) for piece in moved))


def on_device(
    hidden,
    lengths,
    norm_gain,
    w_query,
    key_weight_matrix,
    value_weight_matrix,
    w_out,
    key_cache,
    cached_value_rows,
    next_query,
    upcoming_key_weight,
    upcoming_value_weight,
):
    next_parts = reshard((next_query, upcoming_key_weight, upcoming_value_weight))
    step_count, row_count, width = hidden.shape
    head_size = key_cache.shape[3]
    kv_local = key_cache.shape[1]
    context = key_cache.shape[2]
    query_heads = w_query.shape[1] // head_size
    group = query_heads // kv_local
    scale = 1.0 / math.sqrt(head_size)
    normalized_input = normalize(hidden.reshape(step_count * row_count, width), norm_gain)
    token_positions = jnp.concatenate([lengths + step for step in range(step_count)])
    query_rows = jnp.dot(normalized_input, w_query, preferred_element_type=jnp.float32).reshape(
        step_count * row_count, query_heads, head_size
    )
    query_rows = (
        apply_rotation(query_rows, token_positions)
        .astype(jnp.bfloat16)
        .reshape(step_count, row_count, kv_local, group, head_size)
    )
    current_key_rows = jnp.dot(
        normalized_input, key_weight_matrix, preferred_element_type=jnp.float32
    ).reshape(step_count * row_count, kv_local, head_size)
    current_key_rows = (
        apply_rotation(current_key_rows, token_positions)
        .astype(jnp.bfloat16)
        .reshape(step_count, row_count, kv_local, head_size)
    )
    current_value_rows = jnp.dot(
        normalized_input, value_weight_matrix, preferred_element_type=jnp.float32
    ).astype(jnp.bfloat16)
    current_value_rows = current_value_rows.reshape(step_count, row_count, kv_local, head_size)
    cached = (
        jnp.einsum("srgqd,rgkd->srgqk", query_rows, key_cache, preferred_element_type=jnp.float32)
        * scale
    )
    valid = (jnp.arange(context)[None, :] < lengths[:, None])[None, :, None, None, :]
    cached = jnp.where(valid, cached, -jnp.inf)
    recent = (
        jnp.einsum(
            "srgqd,trgd->srgqt", query_rows, current_key_rows, preferred_element_type=jnp.float32
        )
        * scale
    )
    causal = (jnp.arange(step_count)[None, :] <= jnp.arange(step_count)[:, None])[
        :, None, None, None, :
    ]
    recent = jnp.where(causal, recent, -jnp.inf)
    top = jnp.maximum(
        jnp.max(cached, axis=-1, keepdims=True), jnp.max(recent, axis=-1, keepdims=True)
    )
    cached_exp = jnp.exp(cached - top)
    recent_exp = jnp.exp(recent - top)
    total = jnp.sum(cached_exp, axis=-1, keepdims=True) + jnp.sum(
        recent_exp, axis=-1, keepdims=True
    )
    cached_weight = (cached_exp / total).astype(jnp.bfloat16)
    recent_weight = (recent_exp / total).astype(jnp.bfloat16)
    attended = jnp.einsum(
        "srgqk,rgkd->srgqd", cached_weight, cached_value_rows, preferred_element_type=jnp.float32
    )
    attended = attended + jnp.einsum(
        "srgqt,trgd->srgqd", recent_weight, current_value_rows, preferred_element_type=jnp.float32
    )
    attended = attended.astype(jnp.bfloat16).reshape(
        step_count * row_count, query_heads * head_size
    )
    partial_value = jnp.dot(attended, w_out, preferred_element_type=jnp.float32)
    mixed = lax.psum(partial_value, "tp").astype(jnp.bfloat16).reshape(step_count, row_count, width)
    return (mixed, next_parts[0], next_parts[1], next_parts[2])


def solution(mesh):
    in_specs = (
        P(None, "dp", None),
        P("dp"),
        P(),
        P(None, "tp"),
        P(None, "tp"),
        P(None, "tp"),
        P("tp", None),
        P("dp", "tp", None, None),
        P("dp", "tp", None, None),
        P(("dp", "tp"), None),
        P(("dp", "tp"), None),
        P(("dp", "tp"), None),
    )
    out_specs = (P(None, "dp", None), P("tp", None), P("tp", None), P("tp", None))
    return jax.shard_map(
        on_device, mesh=mesh, in_specs=in_specs, out_specs=out_specs, check_vma=False
    )
```

profile of v0, /device:TPU:0, one launch (start us, length us, event | category | flops | bytes accessed | tf_op | source)
XLA Modules:
  0.0 273.9 jit_solution(4753844468257830550)
XLA Ops:
  7.2 0.0 copy-start
  7.2 0.0 all-gather.6.cloned.1.call-start
  7.2 0.7 all-gather.6.cloned.1.call-update
  7.9 0.0 all-gather.8.cloned.1.call-start
  8.0 0.7 all-gather.8.cloned.1.call-update
  8.7 0.0 all-gather.4.cloned.1.call-start
  8.7 0.7 all-gather.4.cloned.1.call-update
  9.4 1.0 multiply_reduce_fusion
  10.4 47.6 %all-gather.6.cloned.1.call-done = bf16[128,4096]{1,0:T(8,128)(2,1)} async-done(((bf16[8,4096]{1,0:T(8,128)(2,1)}), bf16[128,4096]{1,0:T(8,128)(2,1)}) %all-gather.6.cloned.1.call-update) | async-done | bytes 1048592 | tf_op jit(solution)/shard_map/all_gather | solution.py:39
  57.9 4.3 %all-to-all-start.1 = ((bf16[16,1,8,4096]{3,2,1,0:T(8,128)(2,1)}), bf16[16,1,8,4096]{3,2,1,0:T(8,128)(2,1)S(1)}, u32[]{:S(2)}, u32[]{:S(2)}) async-start(bf16[16,1,8,4096]{3,2,1,0:T(8,128)(2,1)} %bitcast.94), calls=%async_computation.1 | async-start | bytes 2097152 | tf_op jit(solution)/shard_map/all_to_all | solution.py:51
  62.2 1.0 multiply_convert_fusion.1
  63.2 0.1 rsqrt.13
  63.2 0.8 reshape.224
  64.1 0.0 copy-start.4
  64.1 0.0 copy-start.3
  64.2 6.3 %copy.61 = bf16[512,4096]{1,0:T(8,128)(2,1)} copy(bf16[512,4096]{0,1:T(8,128)(2,1)} %bitcast.88) | data formatting | bytes 8388608 | tf_op jit(solution)/shard_map/dot_general | solution.py:81
  70.5 0.1 add_convert_fusion
  70.6 0.3 fusion.29
  70.9 36.4 %all-gather.8.cloned.1.call-done = bf16[128,4096]{1,0:T(8,128)(2,1)} async-done(((bf16[8,4096]{1,0:T(8,128)(2,1)}), bf16[128,4096]{1,0:T(8,128)(2,1)}) %all-gather.8.cloned.1.call-update) | async-done | bytes 1048592 | tf_op jit(solution)/shard_map/all_gather | solution.py:40
  107.3 4.3 %all-to-all-start.2 = ((bf16[16,1,8,4096]{3,2,1,0:T(8,128)(2,1)}), bf16[16,1,8,4096]{3,2,1,0:T(8,128)(2,1)S(1)}, u32[]{:S(2)}, u32[]{:S(2)}) async-start(bf16[16,1,8,4096]{3,2,1,0:T(8,128)(2,1)} %bitcast.93), calls=%async_computation.2 | async-start | bytes 2097152 | tf_op jit(solution)/shard_map/all_to_all | solution.py:51
  111.6 0.1 multiply_cosine_fusion
  111.7 0.1 negate_bitcast_fusion
  111.8 3.4 %fusion.31 = f32[8,4,128]{2,0,1:T(8,128)S(1)} fusion(bf16[8,4096,1]{1,0,2:T(8,128)(2,1)S(1)} %reshape.225, bf16[4,128,4096]{2,1,0:T(8,128)(2,1)} %bitcast.87), kind=kOutput, calls=%fused_computation.56 | convolution fusion | flops 33554432 | bytes 4276224 | tf_op jit(solution)/shard_map/dot_general | solution.py:81
  115.2 0.1 slice_negate_fusion
  115.2 12.6 %all-to-all-done.2 = bf16[16,1,8,4096]{3,2,1,0:T(8,128)(2,1)S(1)} async-done(((bf16[16,1,8,4096]{3,2,1,0:T(8,128)(2,1)}), bf16[16,1,8,4096]{3,2,1,0:T(8,128)(2,1)S(1)}, u32[]{:S(2)}, u32[]{:S(2)}) %all-to-all-start.2) | async-done | bytes 1048608 | tf_op jit(solution)/shard_map/all_to_all | solution.py:51
  127.8 39.9 %all-gather.4.cloned.1.call-done = bf16[512,4096]{1,0:T(8,128)(2,1)} async-done(((bf16[32,4096]{1,0:T(8,128)(2,1)}), bf16[512,4096]{1,0:T(8,128)(2,1)}) %all-gather.4.cloned.1.call-update) | async-done | bytes 4194320 | tf_op jit(solution)/shard_map/all_gather | solution.py:38
  167.7 4.6 %all-to-all-start = ((bf16[16,1,32,4096]{3,2,1,0:T(8,128)(2,1)}), bf16[16,1,32,4096]{3,2,1,0:T(8,128)(2,1)}, u32[]{:S(2)}, u32[]{:S(2)}) async-start(bf16[16,1,32,4096]{3,2,1,0:T(8,128)(2,1)} %bitcast.89), calls=%async_computation | async-start | bytes 8388608 | tf_op jit(solution)/shard_map/all_to_all | solution.py:51
  172.3 0.0 copy-start.2
  172.3 0.1 fusion.23
  172.4 0.1 fusion.15
  172.5 0.2 convolution_multiply_fusion.1
  172.7 0.1 fusion.28
  172.7 0.1 iota_compare_fusion
  172.9 0.0 copy-start.5
  172.9 3.6 %fusion.30 = (f32[2,4,4]{2,0,1:T(2,128)S(1)}, f32[2,4,1,4,4096]{4,3,0,1,2:T(4,128)S(1)}) fusion(bf16[4,1,4096,128]{3,2,1,0:T(8,128)(2,1)} %param.19, bf16[2,4,4,128]{3,1,0,2:T(4,128)(2,1)S(1)} %bitcast.99, pred[4,4096]{1,0:T(4,128)(4,1)S(1)} %iota_compare_fusion), kind=kOutput, calls=%fused_computation.55 | convolution fusion | flops 33947616 | bytes 4743296 | tf_op jit(solution)/shard_map/srgqd,rgkd->srgqk/dot_general | solution.py:102
  176.5 0.1 fusion.21
  176.6 0.3 fusion.11
  176.9 0.1 fusion.25
  177.0 0.3 convolution_convert_fusion
  177.3 0.9 fusion.6
  178.2 0.2 fusion.10
  178.5 0.2 copy-done.1
  178.7 0.6 fusion.16
  179.3 80.5 %all-reduce.1 = bf16[8,4096]{1,0:T(8,128)(2,1)S(1)} all-reduce(f32[8,4096]{1,0:T(8,128)S(1)} %fusion.16), channel_id=1, replica_groups=mesh['dp'=16,'tp'=8] {'tp'}, use_global_device_ids=true, to_apply=%region_5.6 | all-reduce | flops 32768 | bytes 196608 | tf_op jit(solution)/shard_map/psum | solution.py:137
  259.9 0.7 reshape.217
  260.5 1.0 copy.55
  261.6 1.0 copy.56
  262.6 4.7 %copy.54 = bf16[2,8,1,32,4096]{4,3,1,0,2:T(8,128)(2,1)} copy(bf16[2,8,1,32,4096]{4,3,0,1,2:T(8,128)(2,1)} %bitcast.28) | data formatting | bytes 8388608 | tf_op jit(solution)/shard_map/all_to_all | solution.py:51
  (16 shorter events, 0.1 us)
Async XLA Ops:
  7.2 63.4 %copy-start = (bf16[4096,128]{1,0:T(8,128)(2,1)S(1)}, bf16[4096,128]{1,0:T(8,128)(2,1)}, u32[]{:S(2)}) copy-start(bf16[4096,128]{1,0:T(8,128)(2,1)} %param.16) | copy-start | bytes 3145732
  7.2 50.8 %all-gather.6.cloned.1.call-start = ((), (), s32[]{:S(2)}) async-start(), calls=%async_computation.4 | async-start | bytes 1114112 | tf_op jit(solution)/shard_map/all_gather | solution.py:39
  7.9 99.4 %all-gather.8.cloned.1.call-start = ((), (), s32[]{:S(2)}) async-start(), calls=%async_computation.5 | async-start | bytes 1114112 | tf_op jit(solution)/shard_map/all_gather | solution.py:40
  8.7 159.1 %all-gather.4.cloned.1.call-start = ((), (), s32[]{:S(2)}) async-start(), calls=%async_computation.3 | async-start | bytes 4456448 | tf_op jit(solution)/shard_map/all_gather | solution.py:38
  57.9 49.4 %all-to-all-start.1 = ((bf16[16,1,8,4096]{3,2,1,0:T(8,128)(2,1)}), bf16[16,1,8,4096]{3,2,1,0:T(8,128)(2,1)S(1)}, u32[]{:S(2)}, u32[]{:S(2)}) async-start(bf16[16,1,8,4096]{3,2,1,0:T(8,128)(2,1)} %bitcast.94), calls=%async_computation.1 | async-start | bytes 2097152 | tf_op jit(solution)/shard_map/all_to_all | solution.py:51
  64.1 6.4 %copy-start.4 = (s32[4]{0:T(128)S(1)}, s32[4]{0:T(128)}, u32[]{:S(2)}) copy-start(s32[4]{0:T(128)} %param.13) | copy-start | bytes 52
  64.1 6.5 %copy-start.3 = (f32[4096]{0:T(1024)S(1)}, f32[4096]{0:T(1024)}, u32[]{:S(2)}) copy-start(f32[4096]{0:T(1024)} %param.14) | copy-start | bytes 49156
  107.3 20.5 %all-to-all-start.2 = ((bf16[16,1,8,4096]{3,2,1,0:T(8,128)(2,1)}), bf16[16,1,8,4096]{3,2,1,0:T(8,128)(2,1)S(1)}, u32[]{:S(2)}, u32[]{:S(2)}) async-start(bf16[16,1,8,4096]{3,2,1,0:T(8,128)(2,1)} %bitcast.93), calls=%async_computation.2 | async-start | bytes 2097152 | tf_op jit(solution)/shard_map/all_to_all | solution.py:51
  167.7 94.9 %all-to-all-start = ((bf16[16,1,32,4096]{3,2,1,0:T(8,128)(2,1)}), bf16[16,1,32,4096]{3,2,1,0:T(8,128)(2,1)}, u32[]{:S(2)}, u32[]{:S(2)}) async-start(bf16[16,1,32,4096]{3,2,1,0:T(8,128)(2,1)} %bitcast.89), calls=%async_computation | async-start | bytes 8388608 | tf_op jit(solution)/shard_map/all_to_all | solution.py:51
  172.3 4.7 %copy-start.2 = (bf16[4096,128]{1,0:T(8,128)(2,1)S(1)}, bf16[4096,128]{1,0:T(8,128)(2,1)}, u32[]{:S(2)}) copy-start(bf16[4096,128]{1,0:T(8,128)(2,1)} %param.17) | copy-start | bytes 3145732
  172.9 4.5 %copy-start.5 = (bf16[4,1,4096,128]{3,2,1,0:T(8,128)(2,1)S(1)}, bf16[4,1,4096,128]{3,2,1,0:T(8,128)(2,1)}, u32[]{:S(2)}) copy-start(bf16[4,1,4096,128]{3,2,1,0:T(8,128)(2,1)} %param.20) | copy-start | bytes 12582916
  176.5 2.2 copy-start.1
Sparse Core Ops, SparseCore 0:
  10.5 47.4 all-gather.5
  60.4 46.8 all-gather.7
  109.8 57.8 all-gather.3
where the time goes:
time: 275 us; the launch traced here: 274 us
  waiting for transfers between devices  139 us (51%)
  blocking collectives  80.5 us (29%)
  local copies, waits for them, and re-layouts  15 us (5%)
  between operations  13.9 us (5%)
  starting transfers between devices  13.2 us (5%)
  matrix products  9.52 us (3%)
  other arithmetic  3.16 us (1%)
    psum x1, blocking collectives, on_device(): lax.psum(partial_value, 'tp').astype(jnp.bfloat16)  80.5 us
    all_gather x1, waiting for transfers between devices, reshard(): lax.all_gather(weights[1], 'dp', axis=0, tiled=True)  47.6 us
    all_gather x1, waiting for transfers between devices, reshard(): lax.all_gather(weights[0], 'dp', axis=0, tiled=True)  39.9 us
    all_gather x1, waiting for transfers between devices, reshard(): lax.all_gather(weights[2], 'dp', axis=0, tiled=True)  36.4 us
    all_to_all x3, starting transfers between devices, reshard(): lax.all_to_all(as_sent(stacked), 'tp', split_axis=0, concat_axis=1, tiled...  13.1 us
    all_to_all x3, waiting for transfers between devices, reshard(): lax.all_to_all(as_sent(stacked), 'tp', split_axis=0, concat_axis=1, tiled...  12.6 us
    all_to_all x3, local copies, waits for them, and re-layouts, reshard(): lax.all_to_all(as_sent(stacked), 'tp', split_axis=0, concat_axis=1, tiled...  6.78 us
    dot_general x1, local copies, waits for them, and re-layouts, on_device(): jnp.dot(normalized_input, w_query, preferred_element_type=jnp.float32)  6.34 us
  transfers between devices with their start and end apart: 6, of which 4 were waited for; matrix products, arithmetic and copies ran while one was open for 8% of the time, Pallas kernels for 0%

commit v1 on v0

v1 whole, which is shorter than its diff:
```python
import functools
import math

import jax
import jax.numpy as jnp
from jax import lax
from jax.experimental import pallas as pl
from jax.experimental.pallas import tpu as pltpu
from jax.sharding import PartitionSpec as P

MESH = pl.DeviceIdType.MESH
BF = jnp.bfloat16
F32 = jnp.float32

CROSS = 1024
CROSS_PARTS = 2
TURN_PARTS = 6
VMEM_LIMIT = 36 * 2**20
ORDER = (
    0, 18, 9, 24, 1, 54, 55, 2, 19, 30, 56, 10, 11, 25, 36, 57, 3, 4, 58, 59, 5, 20, 60, 61, 62, 31, 42, 63,
    12, 13, 64, 14, 26, 65, 66, 37, 48, 67, 6, 21, 68, 69, 70, 32, 71, 72, 43, 15, 73, 27, 74, 75, 38, 76,
    77, 49, 7, 22, 33, 44, 16, 28, 39, 78, 50, 34, 45, 40, 51, 79, 46, 52, 8, 23, 17, 29, 35, 41, 47, 53,
)


def place():
    dp, tp = lax.axis_index("dp"), lax.axis_index("tp")
    return tp % 4, (dp // 8) * 2 + tp // 4, (dp // 2) % 4, dp % 2


def device(x, y, z, core):
    return ((y // 2) * 8 + z * 2 + core, (y % 2) * 4 + x)


def cut(start, width, parts):
    tiles = width // 128
    edges = [128 * (tiles * i // parts) for i in range(parts + 1)]
    return [(start + edges[i], edges[i + 1] - edges[i]) for i in range(parts)]


class Gather:
    def __init__(self, rows, width):
        self.rows, self.width = rows, width
        cuts = cut(0, CROSS, CROSS_PARTS) + cut(CROSS, width - CROSS, TURN_PARTS)
        self.parts = [(n < CROSS_PARTS, at, size) for n, (at, size) in enumerate(cuts)]
        self.count = len(cuts) * 10

    def scratch(self):
        return [
            pltpu.VMEM((2, self.rows, self.width), BF),
            pltpu.VMEM((4, 2, self.rows, CROSS), BF),
            pltpu.SemaphoreType.DMA((self.count,)),
            pltpu.SemaphoreType.DMA((self.count,)),
        ]

    def begin(self, held, moved, ring, sent, got):
        self.held, self.moved, self.ring, self.sent, self.got = held, moved, ring, sent, got
        self.x, self.y, self.z, self.core = place()
        self.ends = []

    def greetings(self):
        x, y, z, core = self.x, self.y, self.z, self.core
        senders = [device(x, y, (z + i) % 4, core) for i in range(1, 4)]
        senders += [device((x + i) % 4, y, z, core) for i in range(1, 4)]
        senders += [device(x, y, z, 1 - core)]
        near = [device((x + i) % 4, y % 2 * 2 + j, z, core) for i in range(4) for j in range(2)]
        edge = (y == 0) | (y == 3)
        return senders, near, edge

    def send(self, source, target, sent, got, to, when=None):
        copy = pltpu.make_async_remote_copy(
            src_ref=source,
            dst_ref=target,
            send_sem=self.sent.at[sent],
            recv_sem=self.got.at[got],
            device_id=to,
            device_id_type=MESH,
        )
        if when is None:
            copy.start()
            self.ends.append(copy.wait_send)
        else:
            pl.when(when)(copy.start)
            self.ends.append(lambda: pl.when(when)(copy.wait_send))

    def arrive(self, target, got):
        pltpu.make_async_remote_copy(
            src_ref=target,
            dst_ref=target,
            send_sem=self.sent.at[0],
            recv_sem=self.got.at[got],
            device_id=device(self.x, self.y, self.z, 1 - self.core),
            device_id_type=MESH,
        ).wait_recv()

    def z_start(self, view, sent, got):
        own = view(0)
        self.send(own, own, sent, got, device(self.x, self.y, (self.z + 1) % 4, self.core))
        self.send(own, own, sent + 1, got + 1, device(self.x, self.y, (self.z + 3) % 4, self.core))

    def z_pass(self, view, sent, got, upward):
        near, step = (3, 1) if upward else (1, 3)
        piece = view(near)
        self.arrive(piece, got + (0 if upward else 1))
        self.send(piece, piece, sent + 2, got + 2, device(self.x, self.y, (self.z + step) % 4, self.core))

    def z_other(self, view, got, upward):
        self.arrive(view(1 if upward else 3), got + (1 if upward else 0))

    def z_far(self, view, got):
        self.arrive(view(2), got + 2)

    def both(self, view, target, sent, got, x, stays):
        y = self.y
        for which in range(2):
            goal_y = y // 2 + 2 * which
            here = stays & (goal_y == y)
            self.send(view, target, sent + which, got + y % 2, device(x, goal_y, self.z, self.core), jnp.logical_not(here))
            pl.when(here)(pltpu.make_async_copy(view, target, self.sent.at[sent + which]).start)

    def land(self, view, target, slot, sent, got, stays):
        y = self.y
        here = stays & (y % 2 * 2 + slot == y)
        pl.when(here)(pltpu.make_async_copy(view, target, self.sent.at[sent + y // 2]).wait)
        pl.when(jnp.logical_not(here))(lambda: self.arrive(target, got + slot))

    def share(self, whole, sem):
        self.send(whole(self.core), whole(self.core), sem, sem, device(self.x, self.y, self.z, 1 - self.core))

    def cross_steps(self, n):
        at, size = self.parts[n][1:]
        base = n * 10
        upward = n % 2 == 0
        x, y, z, core = self.x, self.y, self.z, self.core
        columns, slots = pl.ds(at, size), pl.ds(0, 2)
        here = jnp.bool_(True)
        first = self.moved.at[0, :, columns]
        view = lambda step: self.ring.at[(z + step) % 4, :, :, columns]
        at_z = lambda to_x: self.ring.at[to_x, :, :, columns]
        final = lambda from_x: self.held.at[core, slots, from_x, :, columns]
        whole = lambda core: self.held.at[core, slots, :, :, columns]

        def start():
            self.both(first, self.ring.at[z, y % 2, :, columns], base, base, x, here)

        def column():
            for slot in range(2):
                self.land(first, self.ring.at[z, slot, :, columns], slot, base, base, here)
            self.z_start(view, base + 2, base + 2)

        def cross(step):
            goal = (z + step) % 4
            hops = (goal - x + 4) % 4
            to = device(goal, y, z, core)
            self.send(at_z(goal), final(x), base + 5 + step, base + 4 + hops, to, hops != 0)
            stay = pltpu.make_async_copy(at_z(goal), final(x), self.sent.at[base + 5 + step])
            pl.when(hops == 0)(stay.start)

        def relay():
            self.z_pass(view, base + 2, base + 2, upward)

        def second():
            self.z_other(view, base + 2, upward)
            cross(1 if upward else 3)

        def far():
            self.z_far(view, base + 2)
            cross(2)

        def finish():
            step = (x - z + 4) % 4
            pltpu.make_async_copy(at_z(x), final(x), self.sent.at[base + 5 + step]).wait()
            for hops in range(1, 4):
                self.arrive(final((x + 4 - hops) % 4), base + 4 + hops)
            self.share(whole, base + 9)

        def done():
            self.arrive(whole(1 - core), base + 9)

        return [
            ("start", start),
            ("column", column),
            ("cross0", functools.partial(cross, 0)),
            ("relay", relay),
            ("cross1", functools.partial(cross, 3 if upward else 1)),
            ("second", second),
            ("far", far),
            ("finish", finish),
            ("done", done),
        ]

    def turn_steps(self, n):
        at, size = self.parts[n][1:]
        base = n * 10
        upward = n % 2 == 0
        x, y, z, core = self.x, self.y, self.z, self.core
        columns, slots = pl.ds(at, size), pl.ds(0, 2)
        shift = (x + n) % 4
        goal = (z + 8 - x - n % 4) % 4
        at_x = lambda step: (z + step + 8 - x - n % 4) % 4
        pair = lambda step: self.held.at[core, slots, at_x(step), :, columns]
        whole = lambda core: self.held.at[core, slots, :, :, columns]
        first, shifted = (self.moved.at[slot, :, columns] for slot in range(2))
        view = self.moved.at[jnp.where(shift == 0, 0, 1), :, columns]

        def start():
            self.send(first, shifted, base, base, device(x, y, (z + shift) % 4, core), shift != 0)

        def turn():
            pl.when(shift != 0)(lambda: self.arrive(shifted, base))
            self.both(view, self.held.at[core, y % 2, x, :, columns], base + 1, base + 1, goal, goal == x)

        def column():
            for slot in range(2):
                target = self.held.at[core, slot, at_x(0), :, columns]
                self.land(view, target, slot, base + 1, base + 1, at_x(0) == x)
            self.z_start(pair, base + 3, base + 3)

        def relay():
            self.z_pass(pair, base + 3, base + 3, upward)

        def finish():
            self.z_other(pair, base + 3, upward)
            self.z_far(pair, base + 3)
            self.share(whole, base + 9)

        def done():
            self.arrive(whole(1 - core), base + 9)

        return [
            ("start", start),
            ("turn", turn),
            ("column", column),
            ("relay", relay),
            ("finish", finish),
            ("done", done),
        ]

    def steps(self):
        steps = {}
        for n, part in enumerate(self.parts):
            made = self.cross_steps(n) if part[0] else self.turn_steps(n)
            steps.update({f"{n}.{name}": step for name, step in made})
        return steps

    def finish(self):
        for end in self.ends:
            end()


def greet(senders, near, edge, loads):
    barrier = pltpu.get_barrier_semaphore()
    me = (lax.axis_index("dp"), lax.axis_index("tp"))
    signal = lambda peer: pl.semaphore_signal(barrier, inc=1, device_id=peer, device_id_type=MESH)
    for peer in senders:
        signal(peer)
    for peer in near:
        pl.when((peer[0] != me[0]) | (peer[1] != me[1]))(functools.partial(signal, peer))
    for load in loads:
        load.wait()
    pl.semaphore_wait(barrier, len(senders) + len(near) - edge.astype(jnp.int32))


class Layer:
    def __init__(self, step_count, row_count, width, group, head, context):
        self.step_count, self.row_count, self.width = step_count, row_count, width
        self.group, self.head, self.context = group, head, context
        self.tokens = step_count * row_count
        self.share = width // 8

    def scratch(self):
        rows, context, head = self.row_count, self.context, self.head
        features = self.group * head
        return [
            pltpu.VMEM((self.width, features), BF),
            pltpu.VMEM((self.width, head), BF),
            pltpu.VMEM((self.width, head), BF),
            pltpu.VMEM((features, self.width), BF),
            pltpu.VMEM((rows, context, head), BF),
            pltpu.VMEM((rows, context, head), BF),
            pltpu.VMEM((8, self.tokens, self.share), F32),
            pltpu.VMEM((8, self.tokens, self.share), F32),
            pltpu.VMEM((8, self.tokens, self.share), F32),
            pltpu.SemaphoreType.DMA((5 + 2 * rows,)),
            pltpu.SemaphoreType.DMA((14,)),
            pltpu.SemaphoreType.DMA((16,)),
        ]

    def begin(self, hidden, lengths, gain, sources, mixed, scratch):
        self.hidden, self.lengths, self.gain = hidden, lengths, gain
        self.w_query, self.w_key, self.w_value, self.w_out = scratch[:4]
        self.keys, self.values, self.partial, self.landed, self.mixed = scratch[4:9]
        loads, self.sent, self.got = scratch[9:]
        self.result = pltpu.make_async_copy(self.mixed, mixed, loads.at[4 + 2 * self.row_count])
        w_query, w_key, w_value, w_out, keys, values = sources
        pairs = [(w_query, self.w_query), (w_key, self.w_key), (w_value, self.w_value)]
        for r in range(self.row_count):
            pairs.append((keys.at[r, 0], self.keys.at[r]))
            pairs.append((values.at[r, 0], self.values.at[r]))
        pairs.append((w_out, self.w_out))
        self.loads = [pltpu.make_async_copy(a, b, loads.at[i]) for i, (a, b) in enumerate(pairs)]
        for load in self.loads:
            load.start()
        self.ends = []
        self.rows = {}

    def normalize(self):
        values = jnp.concatenate([self.hidden[s] for s in range(self.step_count)], axis=0).astype(F32)
        scale = lax.rsqrt(jnp.mean(values * values, axis=-1, keepdims=True) + 1e-06)
        self.normed = (values * scale * self.gain[...]).astype(BF)

    def turn(self):
        steps, rows, half = self.step_count, self.row_count, self.head // 2
        token = lax.broadcasted_iota(jnp.int32, (self.tokens, self.head), 0)
        lane = lax.broadcasted_iota(jnp.int32, (self.tokens, self.head), 1)
        position = token // rows
        for r in range(rows):
            position = position + jnp.where(token % rows == r, self.lengths[r], 0)
        power = (lane % half).astype(F32) * (2.0 / self.head)
        angles = position.astype(F32) * jnp.exp(-power * math.log(1000000.0))
        self.cosine = jnp.cos(angles)
        sine = jnp.sin(angles)
        self.sine = jnp.where(lane < half, -sine, sine)

    def rotate(self, vectors):
        return (vectors * self.cosine + pltpu.roll(vectors, self.head // 2, 1) * self.sine).astype(BF)

    def project_query(self, g):
        if g == 0:
            self.loads[0].wait()
            self.query = []
        at = g * self.head
        wide = jnp.dot(self.normed, self.w_query[:, at : at + self.head], preferred_element_type=F32)
        self.query.append(self.rotate(wide))

    def project_query_pair(self, g):
        if g == 0:
            self.loads[0].wait()
            self.query = []
        at = g * self.head
        wide = jnp.dot(self.normed, self.w_query[:, at : at + 2 * self.head], preferred_element_type=F32)
        self.query.append(self.rotate(wide[:, : self.head]))
        self.query.append(self.rotate(wide[:, self.head :]))

    def project_key(self):
        self.loads[1].wait()
        self.fresh_key = self.rotate(jnp.dot(self.normed, self.w_key[...], preferred_element_type=F32))

    def project_value(self):
        self.loads[2].wait()
        self.fresh_value = jnp.dot(self.normed, self.w_value[...], preferred_element_type=F32).astype(BF)

    def pick(self, size, total, test):
        out = lax.broadcasted_iota(jnp.int32, (size, total), 0)
        inner = lax.broadcasted_iota(jnp.int32, (size, total), 1)
        return test(out, inner).astype(F32).astype(BF)

    def score(self, r):
        self.loads[3 + 2 * r].wait()
        steps, rows, tokens = self.step_count, self.row_count, self.tokens
        heads = self.group * steps
        every = jnp.concatenate(self.query, axis=0)
        chosen = self.pick(
            heads, self.group * tokens, lambda o, i: i == (o // steps) * tokens + (o % steps) * rows + r
        )
        query = jnp.dot(chosen, every, preferred_element_type=F32).astype(BF)
        scale = 1.0 / math.sqrt(self.head)
        along = (((1,), (1,)), ((), ()))
        cached = lax.dot_general(query, self.keys[r], along, preferred_element_type=F32) * scale
        slot = lax.broadcasted_iota(jnp.int32, cached.shape, 1)
        cached = jnp.where(slot < self.lengths[r], cached, -jnp.inf)
        recent = lax.dot_general(query, self.fresh_key, along, preferred_element_type=F32) * scale
        out = lax.broadcasted_iota(jnp.int32, recent.shape, 0)
        token = lax.broadcasted_iota(jnp.int32, recent.shape, 1)
        recent = jnp.where((token % rows == r) & (token // rows <= out % steps), recent, -jnp.inf)
        top = jnp.maximum(
            jnp.max(cached, axis=-1, keepdims=True), jnp.max(recent, axis=-1, keepdims=True)
        )
        cached_exp = jnp.exp(cached - top)
        recent_exp = jnp.exp(recent - top)
        total = jnp.sum(cached_exp, axis=-1, keepdims=True) + jnp.sum(recent_exp, axis=-1, keepdims=True)
        self.rows[r] = (cached_exp / total).astype(BF), (recent_exp / total).astype(BF)

    def attend(self, r):
        self.loads[4 + 2 * r].wait()
        cached, recent = self.rows[r]
        result = jnp.dot(cached, self.values[r], preferred_element_type=F32)
        result = result + jnp.dot(recent, self.fresh_value, preferred_element_type=F32)
        self.rows[r] = result.astype(BF)

    def lay_out(self):
        steps, rows, tokens = self.step_count, self.row_count, self.tokens
        heads = self.group * steps
        every = jnp.concatenate([self.rows[r] for r in range(rows)], axis=0)
        parts = []
        for g in range(self.group):
            chosen = self.pick(
                tokens, rows * heads, lambda o, i: i == (o % rows) * heads + g * steps + o // rows
            )
            parts.append(jnp.dot(chosen, every, preferred_element_type=F32).astype(BF))
        self.attended = jnp.concatenate(parts, axis=1)

    def project_out(self, t):
        if t == 0:
            self.loads[-1].wait()
        columns = slice(t * self.share, (t + 1) * self.share)
        self.partial[t] = jnp.dot(self.attended, self.w_out[:, columns], preferred_element_type=F32)

    def group_peers(self):
        dp, tp = lax.axis_index("dp"), lax.axis_index("tp")
        return [(dp, (tp + step) % 8) for step in range(1, 8)]

    def copy(self, source, target, sent, got, to):
        return pltpu.make_async_remote_copy(
            src_ref=source,
            dst_ref=target,
            send_sem=self.sent.at[sent],
            recv_sem=self.got.at[got],
            device_id=to,
            device_id_type=MESH,
        )

    def scatter(self):
        me = lax.axis_index("tp")
        for step, peer in enumerate(self.group_peers(), 1):
            copy = self.copy(self.partial.at[peer[1]], self.landed.at[step], step - 1, step, peer)
            copy.start()
            self.ends.append(copy.wait_send)

    def gather(self):
        me = lax.axis_index("tp")
        total = self.partial[me]
        for step, peer in enumerate(self.group_peers(), 1):
            self.copy(self.landed.at[step], self.landed.at[step], 0, step, peer).wait_recv()
            total = total + self.landed[step]
        self.mixed[me] = total
        for step, peer in enumerate(self.group_peers(), 1):
            copy = self.copy(self.mixed.at[me], self.mixed.at[me], 6 + step, 8 + step, peer)
            copy.start()
            self.ends.append(copy.wait_send)

    def collect(self):
        me = lax.axis_index("tp")
        for step, peer in enumerate(self.group_peers(), 1):
            owner = (me + 8 - step) % 8
            self.copy(self.mixed.at[owner], self.mixed.at[owner], 0, 8 + step, peer).wait_recv()
        self.result.start()
        self.ends.append(self.result.wait)

    def steps(self):
        steps = {"normalize": self.normalize, "turn": self.turn}
        for g in range(0, self.group, 2):
            steps[f"query{g}"] = functools.partial(self.project_query_pair, g)
        steps["key"] = self.project_key
        steps["value"] = self.project_value
        for r in range(self.row_count):
            steps[f"score{r}"] = functools.partial(self.score, r)
            steps[f"attend{r}"] = functools.partial(self.attend, r)
        steps["lay_out"] = self.lay_out
        for t in range(8):
            steps[f"out{t}"] = functools.partial(self.project_out, t)
        steps["scatter"] = self.scatter
        steps["gather"] = self.gather
        steps["collect"] = self.collect
        return steps

    def finish(self):
        for end in self.ends:
            end()


def kernel(gather, layer, *refs):
    lengths, hidden, gain, q, k, v = refs[:6]
    sources, (held, mixed) = refs[6:12], refs[12:14]
    moved, ring, small, sent, got, own, hidden_here, gain_here, lengths_here = refs[14:23]
    gather.begin(held, moved, ring, sent, got)
    high, low = q.shape[0], k.shape[0]
    pairs = [
        (q, moved.at[0, pl.ds(0, high), :]),
        (k, small.at[0]),
        (v, small.at[1]),
        (hidden, hidden_here),
        (gain, gain_here),
        (lengths, lengths_here),
    ]
    loads = [pltpu.make_async_copy(a, b, own.at[i]) for i, (a, b) in enumerate(pairs)]
    for load in loads:
        load.start()
    layer.begin(hidden_here, lengths_here, gain_here, sources, mixed, refs[23:])
    senders, near, edge = gather.greetings()
    greet(senders + layer.group_peers(), near, edge, loads)
    moved[0, pl.ds(high, 2 * low), :] = jnp.concatenate([small[0], small[1]], axis=0)
    steps = [*gather.steps().values(), *layer.steps().values()]
    for number in ORDER:
        steps[number]()
    gather.finish()
    layer.finish()


def write_out(held, mixed, q, k, v, out, low_k, low_v, sems):
    high, low = q.shape[3], k.shape[2] // 4
    copies = [pltpu.make_async_copy(held.at[:, :, :, pl.ds(0, high), :], q, sems.at[0])]
    copies[0].start()
    for at, (staged, target) in enumerate(((low_k, k), (low_v, v))):
        for core in range(2):
            for slot in range(2):
                rows = slice(high + at * low, high + (at + 1) * low)
                staged[core, slot] = jnp.concatenate([held[core, slot, x, rows, :] for x in range(4)], axis=0)
        copies.append(pltpu.make_async_copy(staged, target, sems.at[1 + at]))
        copies[-1].start()
    steps, rows, _ = out.shape
    share = mixed.shape[2]
    for t in range(mixed.shape[0]):
        for s in range(steps):
            out[s, :, t * share : (t + 1) * share] = mixed[t, s * rows : (s + 1) * rows, :].astype(BF)
    for copy in copies:
        copy.wait()


def on_device(
    hidden,
    lengths,
    norm_gain,
    w_query,
    key_weight_matrix,
    value_weight_matrix,
    w_out,
    key_cache,
    cached_value_rows,
    next_query,
    upcoming_key_weight,
    upcoming_value_weight,
):
    step_count, row_count, width = hidden.shape
    head = key_cache.shape[3]
    group = w_query.shape[1] // head
    context = key_cache.shape[2]
    tokens = step_count * row_count
    high, low = next_query.shape[0], upcoming_key_weight.shape[0]
    rows = high + 2 * low
    gather = Gather(rows, width)
    layer = Layer(step_count, row_count, width, group, head, context)
    vmem = pl.BlockSpec(memory_space=pltpu.VMEM)
    hbm = pl.BlockSpec(memory_space=pltpu.HBM)
    held, mixed = pl.pallas_call(
        functools.partial(kernel, gather, layer),
        out_shape=(
            jax.ShapeDtypeStruct((2, 2, 4, rows, width), BF),
            jax.ShapeDtypeStruct((8, tokens, width // 8), F32),
        ),
        in_specs=[hbm] * 12,
        out_specs=(pl.BlockSpec(memory_space=pl.ANY),) * 2,
        scratch_shapes=[
            *gather.scratch()[:2],
            pltpu.VMEM((2, low, width), BF),
            *gather.scratch()[2:],
            pltpu.SemaphoreType.DMA((6,)),
            pltpu.VMEM((step_count, row_count, width), BF),
            pltpu.VMEM((1, width), F32),
            pltpu.SMEM((row_count,), jnp.int32),
            *layer.scratch(),
        ],
        compiler_params=pltpu.CompilerParams(
            collective_id=0, has_side_effects=True, vmem_limit_bytes=VMEM_LIMIT
        ),
        cost_estimate=pl.CostEstimate(flops=10**9, bytes_accessed=40 * 2**20, transcendentals=10**5),
    )(
        *(
            pltpu.with_memory_space_constraint(each, pltpu.HBM)
            for each in (
                lengths,
                hidden,
                norm_gain.reshape(1, width),
                next_query,
                upcoming_key_weight,
                upcoming_value_weight,
                w_query,
                key_weight_matrix,
                value_weight_matrix,
                w_out,
                key_cache,
                cached_value_rows,
            )
        ),
    )
    q, k, v, mixed = pl.pallas_call(
        write_out,
        out_shape=(
            jax.ShapeDtypeStruct((2, 2, 4, high, width), BF),
            jax.ShapeDtypeStruct((2, 2, 4 * low, width), BF),
            jax.ShapeDtypeStruct((2, 2, 4 * low, width), BF),
            jax.ShapeDtypeStruct((step_count, row_count, width), BF),
        ),
        in_specs=[vmem] * 2,
        out_specs=(hbm, hbm, hbm, vmem),
        scratch_shapes=[
            pltpu.VMEM((2, 2, 4 * low, width), BF),
            pltpu.VMEM((2, 2, 4 * low, width), BF),
            pltpu.SemaphoreType.DMA((3,)),
        ],
        compiler_params=pltpu.CompilerParams(vmem_limit_bytes=16 * 2**20),
    )(
        pltpu.with_memory_space_constraint(held, pltpu.VMEM),
        pltpu.with_memory_space_constraint(mixed, pltpu.VMEM),
    )
    return mixed, q.reshape(-1, width), k.reshape(-1, width), v.reshape(-1, width)


def solution(mesh):
    in_specs = (
        P(None, "dp", None),
        P("dp"),
        P(),
        P(None, "tp"),
        P(None, "tp"),
        P(None, "tp"),
        P("tp", None),
        P("dp", "tp", None, None),
        P("dp", "tp", None, None),
        P(("dp", "tp"), None),
        P(("dp", "tp"), None),
        P(("dp", "tp"), None),
    )
    out_specs = (P(None, "dp", None), P("tp", None), P("tp", None), P("tp", None))
    return jax.shard_map(
        on_device, mesh=mesh, in_specs=in_specs, out_specs=out_specs, check_vma=False
    )
```

time: 275 us -> 56.9 us (0.21)
  the two profiles are of different devices: /device:TPU:0 before, /device:TPU:1 now
where the time goes in v1:
time: 56.9 us; the launch traced here: 55.9 us
  Pallas kernels  55.2 us (97%)
  between operations  0.64 us (1%)
    pallas_call x1, Pallas kernels, on_device(): pl.pallas_call(functools.partial(kernel, gather, layer), out_shape=(jax.S...  51.9 us
    pallas_call x1, Pallas kernels, on_device(): pl.pallas_call(write_out, out_shape=(jax.ShapeDtypeStruct((2, 2, 4, high,...  3.32 us

profile of v1, /device:TPU:1, one launch (start us, length us, event | category | flops | bytes accessed | tf_op | source)
XLA Modules:
  0.0 55.9 jit_solution(10057568907733447109)
XLA Ops:
  0.6 51.9 %shard_map.147 = (bf16[2,2,4,48,4096]{4,3,2,1,0:T(8,128)(2,1)S(1)}, f32[8,8,512]{2,1,0:T(8,128)S(1)}) custom-call(s32[4]{0:T(128)} %refs_0_.1, bf16[2,4,4096]{2,1,0:T(4,128)(2,1)} %refs_1_.1, f32[1,4096]{1,0:T(1,128)} %bitcast.4, bf16[32,4096]{1,0:T(8,128)(2,1)} %refs_3_.1, bf16[8,4096]{1,0:T(8,128)(2,1)} %refs_4_.1, bf16[8,4096]{1,0:T(8,128)(2,1)} %refs_5_.1, ...), custom_call_target="tpu_custom_call" | custom-call | flops 1000000000 | bytes 41943040 | tf_op jit(solution)/shard_map/pallas_call | solution.py:545
  52.6 3.3 %shard_map.148 = (bf16[2,2,4,32,4096]{4,3,2,1,0:T(8,128)(2,1)}, bf16[2,2,32,4096]{3,2,1,0:T(8,128)(2,1)}, bf16[2,2,32,4096]{3,2,1,0:T(8,128)(2,1)}, bf16[2,4,4096]{2,1,0:T(4,128)(2,1)}) custom-call(bf16[2,2,4,48,4096]{4,3,2,1,0:T(8,128)(2,1)S(1)} %get-tuple-element.10.held, f32[8,8,512]{2,1,0:T(8,128)S(1)} %get-tuple-element.11.mixed), custom_call_target="tpu_custom_call" | custom-call | tf_op jit(solution)/shard_map/pallas_call | solution.py:586

commit v2 on v1

--- a/solution.py
+++ b/solution.py
@@ -12,14 +12,18 @@
 BF = jnp.bfloat16
 F32 = jnp.float32
 
-CROSS = 1024
+CROSS = 768
+TURN = 2304
 CROSS_PARTS = 2
-TURN_PARTS = 6
+TURN_PARTS = 4
+LATE_PARTS = 3
 VMEM_LIMIT = 36 * 2**20
 ORDER = (
-    0, 18, 9, 24, 1, 54, 55, 2, 19, 30, 56, 10, 11, 25, 36, 57, 3, 4, 58, 59, 5, 20, 60, 61, 62, 31, 42, 63,
-    12, 13, 64, 14, 26, 65, 66, 37, 48, 67, 6, 21, 68, 69, 70, 32, 71, 72, 43, 15, 73, 27, 74, 75, 38, 76,
-    77, 49, 7, 22, 33, 44, 16, 28, 39, 78, 50, 34, 45, 40, 51, 79, 46, 52, 8, 23, 17, 29, 35, 41, 47, 53,
+    42, 0, 56, 9, 70, 43, 84, 85, 18, 57, 86, 1, 24, 2, 44, 87, 71, 45, 10, 30, 11, 3, 88, 89, 19, 90, 58, 4,
+    59, 5, 36, 91, 12, 92, 93, 25, 94, 46, 72, 13, 47, 95, 73, 48, 14, 50, 20, 96, 97, 31, 98, 60, 61, 62,
+    64, 26, 99, 100, 101, 102, 6, 37, 103, 49, 74, 75, 76, 51, 52, 78, 104, 32, 105, 106, 15, 21, 63, 65, 66,
+    107, 38, 27, 77, 79, 80, 7, 33, 53, 16, 22, 108, 39, 67, 28, 54, 81, 34, 68, 109, 40, 82, 8, 17, 23, 29,
+    35, 41, 55, 69, 83,
 )
 
 
@@ -41,31 +45,46 @@
 class Gather:
     def __init__(self, rows, width):
         self.rows, self.width = rows, width
-        cuts = cut(0, CROSS, CROSS_PARTS) + cut(CROSS, width - CROSS, TURN_PARTS)
-        self.parts = [(n < CROSS_PARTS, at, size) for n, (at, size) in enumerate(cuts)]
-        self.count = len(cuts) * 10
+        bounds = [(0, CROSS, CROSS_PARTS), (CROSS, TURN, TURN_PARTS)]
+        self.late_at = CROSS + TURN
+        bounds.append((self.late_at, width - self.late_at, LATE_PARTS))
+        self.parts = [(kind, at, size) for kind, bound in enumerate(bounds) for at, size in cut(*bound)]
+        self.count = len(self.parts) * 19
 
     def scratch(self):
         return [
             pltpu.VMEM((2, self.rows, self.width), BF),
             pltpu.VMEM((4, 2, self.rows, CROSS), BF),
+            pltpu.VMEM((2, 4, self.rows, self.width - self.late_at), BF),
             pltpu.SemaphoreType.DMA((self.count,)),
             pltpu.SemaphoreType.DMA((self.count,)),
         ]
 
-    def begin(self, held, moved, ring, sent, got):
-        self.held, self.moved, self.ring, self.sent, self.got = held, moved, ring, sent, got
+    def begin(self, held, moved, ring, late, sent, got):
+        self.held, self.moved, self.ring, self.late, self.sent, self.got = held, moved, ring, late, sent, got
         self.x, self.y, self.z, self.core = place()
+        self.edge = (self.y == 0) | (self.y == 3)
+        self.middle = jnp.logical_not(self.edge)
         self.ends = []
 
-    def greetings(self):
+    def greet(self, loads):
         x, y, z, core = self.x, self.y, self.z, self.core
-        senders = [device(x, y, (z + i) % 4, core) for i in range(1, 4)]
-        senders += [device((x + i) % 4, y, z, core) for i in range(1, 4)]
-        senders += [device(x, y, z, 1 - core)]
-        near = [device((x + i) % 4, y % 2 * 2 + j, z, core) for i in range(4) for j in range(2)]
-        edge = (y == 0) | (y == 3)
-        return senders, near, edge
+        barrier = pltpu.get_barrier_semaphore()
+
+        def signal(peers):
+            for peer in peers:
+                pl.semaphore_signal(barrier, inc=1, device_id=peer, device_id_type=MESH)
+
+        def row(at_y, first=0):
+            return [device((x + i) % 4, at_y, z, core) for i in range(first, 4)]
+
+        signal([device(x, y, (z + i) % 4, core) for i in range(1, 4)] + [device(x, y, z, 1 - core)])
+        signal(row(y, 1) + row(y // 2 * 2 + 1 - y % 2))
+        pl.when(self.edge)(lambda: signal([device(x, 3 - y, z, core)]))
+        pl.when(self.middle)(lambda: signal(row(y % 2 * 2) + row(y % 2 * 2 + 1)))
+        for load in loads:
+            load.wait()
+        pl.semaphore_wait(barrier, 15 + self.edge.astype(jnp.int32))
 
     def send(self, source, target, sent, got, to, when=None):
         copy = pltpu.make_async_remote_copy(
@@ -129,7 +148,7 @@
 
     def cross_steps(self, n):
         at, size = self.parts[n][1:]
-        base = n * 10
+        base = n * 19
         upward = n % 2 == 0
         x, y, z, core = self.x, self.y, self.z, self.core
         columns, slots = pl.ds(at, size), pl.ds(0, 2)
@@ -191,7 +210,7 @@
 
     def turn_steps(self, n):
         at, size = self.parts[n][1:]
-        base = n * 10
+        base = n * 19
         upward = n % 2 == 0
         x, y, z, core = self.x, self.y, self.z, self.core
         columns, slots = pl.ds(at, size), pl.ds(0, 2)
@@ -236,29 +255,114 @@
             ("done", done),
         ]
 
+    def late_steps(self, n):
+        at, size = self.parts[n][1:]
+        base = n * 19
+        upward = n % 2 == 0
+        x, y, z, core = self.x, self.y, self.z, self.core
+        columns, local, slots = pl.ds(at, size), pl.ds(at - self.late_at, size), pl.ds(0, 2)
+        shift = (x + n) % 4
+        goal = (z + 8 - x - n % 4) % 4
+        at_x = lambda step: (z + step + 8 - x - n % 4) % 4
+        own = lambda step: self.late.at[0, at_x(step), :, local]
+        passing = lambda step: self.late.at[1, at_x(step), :, local]
+        piece = lambda slot, step: self.held.at[core, slot, at_x(step), :, columns]
+        whole = lambda core: self.held.at[core, slots, :, :, columns]
+        first, shifted = (self.moved.at[slot, :, columns] for slot in range(2))
+        view = self.moved.at[jnp.where(shift == 0, 0, 1), :, columns]
+        inner = jnp.where((y == 0) | (y == 2), 1, 2)
+        slot = jnp.where((y == 0) | (y == 1), 1, 0)
+        keep = pltpu.make_async_copy(
+            self.late.at[0, :, :, local], self.held.at[core, y // 3, :, :, columns], self.sent.at[base + 17]
+        )
+
+        def start():
+            self.send(first, shifted, base, base, device(x, y, (z + shift) % 4, core), shift != 0)
+
+        def turn():
+            pl.when(shift != 0)(lambda: self.arrive(shifted, base))
+            target = self.late.at[0, x, :, local]
+            self.send(view, target, base + 1, base + 1, device(goal, y, z, core), goal != x)
+            pl.when(goal == x)(pltpu.make_async_copy(view, target, self.sent.at[base + 1]).start)
+
+        def column():
+            pl.when(goal == x)(pltpu.make_async_copy(view, own(0), self.sent.at[base + 1]).wait)
+            pl.when(goal != x)(lambda: self.arrive(own(0), base + 1))
+            self.z_start(own, base + 2, base + 2)
+
+        def spread(step):
+            sem = base + 5 + step
+            self.send(own(step), passing(step), sem, base + 13 + step, device(x, 3 - y, z, core), self.edge)
+            got = base + 5 + 4 * slot + step
+            outer = device(x, y // 2 * 3, z, core)
+            self.send(own(step), piece(slot, step), sem, got, outer, self.middle)
+            self.send(own(step), piece(slot, step), sem + 4, got, device(x, inner, z, core), self.middle)
+
+        def passed(step):
+            pl.when(self.edge)(lambda: self.arrive(passing(step), base + 13 + step))
+            got = base + 5 + 4 * slot + step
+            self.send(passing(step), piece(slot, step), base + 9 + step, got, device(x, inner, z, core), self.edge)
+
+        def relay():
+            self.z_pass(own, base + 2, base + 2, upward)
+
+        def second():
+            self.z_other(own, base + 2, upward)
+            spread(1 if upward else 3)
+
+        def far():
+            self.z_far(own, base + 2)
+            spread(2)
+            pl.when(self.edge)(keep.start)
+
+        def finish():
+            def arrived(slot):
+                for step in range(4):
+                    self.arrive(piece(slot, step), base + 5 + 4 * slot + step)
+
+            def at_edge():
+                arrived(1 - y // 3)
+                keep.wait()
+
+            def at_middle():
+                arrived(0)
+                arrived(1)
+
+            pl.when(self.edge)(at_edge)
+            pl.when(self.middle)(at_middle)
+            self.share(whole, base + 18)
+
+        def done():
+            self.arrive(whole(1 - core), base + 18)
+
+        near = 3 if upward else 1
+        return [
+            ("start", start),
+            ("turn", turn),
+            ("column", column),
+            ("spread0", functools.partial(spread, 0)),
+            ("relay", relay),
+            ("spread1", functools.partial(spread, near)),
+            ("second", second),
+            ("far", far),
+            ("passed0", functools.partial(passed, 0)),
+            ("passed1", functools.partial(passed, near)),
+            ("passed2", functools.partial(passed, 4 - near)),
+            ("passed3", functools.partial(passed, 2)),
+            ("finish", finish),
+            ("done", done),
+        ]
+
     def steps(self):
         steps = {}
         for n, part in enumerate(self.parts):
-            made = self.cross_steps(n) if part[0] else self.turn_steps(n)
+            made = (self.cross_steps, self.turn_steps, self.late_steps)[part[0]](n)
             steps.update({f"{n}.{name}": step for name, step in made})
         return steps
 
     def finish(self):
         for end in self.ends:
             end()
-
-
-def greet(senders, near, edge, loads):
-    barrier = pltpu.get_barrier_semaphore()
-    me = (lax.axis_index("dp"), lax.axis_index("tp"))
-    signal = lambda peer: pl.semaphore_signal(barrier, inc=1, device_id=peer, device_id_type=MESH)
-    for peer in senders:
-        signal(peer)
-    for peer in near:
-        pl.when((peer[0] != me[0]) | (peer[1] != me[1]))(functools.partial(signal, peer))
-    for load in loads:
-        load.wait()
-    pl.semaphore_wait(barrier, len(senders) + len(near) - edge.astype(jnp.int32))
 
 
 class Layer:
@@ -472,8 +576,8 @@
 def kernel(gather, layer, *refs):
     lengths, hidden, gain, q, k, v = refs[:6]
     sources, (held, mixed) = refs[6:12], refs[12:14]
-    moved, ring, small, sent, got, own, hidden_here, gain_here, lengths_here = refs[14:23]
-    gather.begin(held, moved, ring, sent, got)
+    moved, ring, late, small, sent, got, own, hidden_here, gain_here, lengths_here = refs[14:24]
+    gather.begin(held, moved, ring, late, sent, got)
     high, low = q.shape[0], k.shape[0]
     pairs = [
         (q, moved.at[0, pl.ds(0, high), :]),
@@ -486,9 +590,8 @@
     loads = [pltpu.make_async_copy(a, b, own.at[i]) for i, (a, b) in enumerate(pairs)]
     for load in loads:
         load.start()
-    layer.begin(hidden_here, lengths_here, gain_here, sources, mixed, refs[23:])
-    senders, near, edge = gather.greetings()
-    greet(senders + layer.group_peers(), near, edge, loads)
+    layer.begin(hidden_here, lengths_here, gain_here, sources, mixed, refs[24:])
+    gather.greet(loads)
     moved[0, pl.ds(high, 2 * low), :] = jnp.concatenate([small[0], small[1]], axis=0)
     steps = [*gather.steps().values(), *layer.steps().values()]
     for number in ORDER:
@@ -501,13 +604,14 @@
     high, low = q.shape[3], k.shape[2] // 4
     copies = [pltpu.make_async_copy(held.at[:, :, :, pl.ds(0, high), :], q, sems.at[0])]
     copies[0].start()
-    for at, (staged, target) in enumerate(((low_k, k), (low_v, v))):
-        for core in range(2):
-            for slot in range(2):
+    for core in range(2):
+        for slot in range(2):
+            for at, (staged, target) in enumerate(((low_k, k), (low_v, v))):
                 rows = slice(high + at * low, high + (at + 1) * low)
                 staged[core, slot] = jnp.concatenate([held[core, slot, x, rows, :] for x in range(4)], axis=0)
-        copies.append(pltpu.make_async_copy(staged, target, sems.at[1 + at]))
-        copies[-1].start()
+                part = (core, slot)
+                copies.append(pltpu.make_async_copy(staged.at[part], target.at[part], sems.at[len(copies)]))
+                copies[-1].start()
     steps, rows, _ = out.shape
     share = mixed.shape[2]
     for t in range(mixed.shape[0]):
@@ -551,9 +655,9 @@
         in_specs=[hbm] * 12,
         out_specs=(pl.BlockSpec(memory_space=pl.ANY),) * 2,
         scratch_shapes=[
-            *gather.scratch()[:2],
+            *gather.scratch()[:3],
             pltpu.VMEM((2, low, width), BF),
-            *gather.scratch()[2:],
+            *gather.scratch()[3:],
             pltpu.SemaphoreType.DMA((6,)),
             pltpu.VMEM((step_count, row_count, width), BF),
             pltpu.VMEM((1, width), F32),
@@ -596,7 +700,7 @@
         scratch_shapes=[
             pltpu.VMEM((2, 2, 4 * low, width), BF),
             pltpu.VMEM((2, 2, 4 * low, width), BF),
-            pltpu.SemaphoreType.DMA((3,)),
+            pltpu.SemaphoreType.DMA((9,)),
         ],
         compiler_params=pltpu.CompilerParams(vmem_limit_bytes=16 * 2**20),
     )(

time: 56.9 us -> 53.8 us (0.946); the launches traced: 55.9 us -> 53.7 us
  Pallas kernels: 55.2 us -> 53.1 us
    pallas_call x1, Pallas kernels: 51.9 us -> 49.7 us  [on_device(): pl.pallas_call(functools.partial(kernel, gather, layer), out_shape=(jax.S...]
where the time goes in v2:
time: 53.8 us; the launch traced here: 53.7 us
  Pallas kernels  53.1 us (99%)
  between operations  0.64 us (1%)
    pallas_call x1, Pallas kernels, on_device(): pl.pallas_call(functools.partial(kernel, gather, layer), out_shape=(jax.S...  49.7 us
    pallas_call x1, Pallas kernels, on_device(): pl.pallas_call(write_out, out_shape=(jax.ShapeDtypeStruct((2, 2, 4, high,...  3.34 us

profile of v2, /device:TPU:1, one launch (start us, length us, event | category | flops | bytes accessed | tf_op | source)
XLA Modules:
  0.0 53.7 jit_solution(8833591021834930901)
XLA Ops:
  0.6 49.7 %shard_map.147 = (bf16[2,2,4,48,4096]{4,3,2,1,0:T(8,128)(2,1)S(1)}, f32[8,8,512]{2,1,0:T(8,128)S(1)}) custom-call(s32[4]{0:T(128)} %refs_0_.1, bf16[2,4,4096]{2,1,0:T(4,128)(2,1)} %refs_1_.1, f32[1,4096]{1,0:T(1,128)} %bitcast.4, bf16[32,4096]{1,0:T(8,128)(2,1)} %refs_3_.1, bf16[8,4096]{1,0:T(8,128)(2,1)} %refs_4_.1, bf16[8,4096]{1,0:T(8,128)(2,1)} %refs_5_.1, ...), custom_call_target="tpu_custom_call" | custom-call | flops 1000000000 | bytes 41943040 | tf_op jit(solution)/shard_map/pallas_call | solution.py:649
  50.4 3.3 %shard_map.148 = (bf16[2,2,4,32,4096]{4,3,2,1,0:T(8,128)(2,1)}, bf16[2,2,32,4096]{3,2,1,0:T(8,128)(2,1)}, bf16[2,2,32,4096]{3,2,1,0:T(8,128)(2,1)}, bf16[2,4,4096]{2,1,0:T(4,128)(2,1)}) custom-call(bf16[2,2,4,48,4096]{4,3,2,1,0:T(8,128)(2,1)S(1)} %get-tuple-element.10.held, f32[8,8,512]{2,1,0:T(8,128)S(1)} %get-tuple-element.11.mixed), custom_call_target="tpu_custom_call" | custom-call | tf_op jit(solution)/shard_map/pallas_call | solution.py:690

commit v3 on v2

--- a/solution.py
+++ b/solution.py
@@ -12,17 +12,17 @@
 BF = jnp.bfloat16
 F32 = jnp.float32
 
-CROSS = 768
-TURN = 2304
+CROSS = 640
+TURN = 2432
 CROSS_PARTS = 2
 TURN_PARTS = 4
 LATE_PARTS = 3
 VMEM_LIMIT = 36 * 2**20
 ORDER = (
-    42, 0, 56, 9, 70, 43, 84, 85, 18, 57, 86, 1, 24, 2, 44, 87, 71, 45, 10, 30, 11, 3, 88, 89, 19, 90, 58, 4,
-    59, 5, 36, 91, 12, 92, 93, 25, 94, 46, 72, 13, 47, 95, 73, 48, 14, 50, 20, 96, 97, 31, 98, 60, 61, 62,
-    64, 26, 99, 100, 101, 102, 6, 37, 103, 49, 74, 75, 76, 51, 52, 78, 104, 32, 105, 106, 15, 21, 63, 65, 66,
-    107, 38, 27, 77, 79, 80, 7, 33, 53, 16, 22, 108, 39, 67, 28, 54, 81, 34, 68, 109, 40, 82, 8, 17, 23, 29,
+    42, 0, 56, 9, 70, 18, 43, 84, 85, 24, 57, 86, 1, 30, 2, 44, 87, 45, 71, 10, 19, 36, 11, 58, 88, 89, 59,
+    3, 4, 5, 25, 90, 46, 72, 91, 47, 73, 48, 50, 92, 12, 93, 20, 13, 94, 95, 14, 31, 60, 96, 61, 62, 64, 26,
+    97, 98, 99, 37, 49, 100, 74, 75, 76, 51, 52, 78, 101, 6, 32, 102, 103, 104, 21, 63, 65, 66, 105, 15, 38,
+    106, 107, 27, 77, 79, 80, 53, 7, 33, 67, 16, 22, 108, 39, 54, 81, 28, 68, 34, 82, 40, 109, 8, 17, 23, 29,
     35, 41, 55, 69, 83,
 )
 

time: 53.8 us -> 51 us (0.948)
  Pallas kernels: 53.1 us -> 50.3 us
    pallas_call x1, Pallas kernels: 49.7 us -> 46.9 us  [on_device(): pl.pallas_call(functools.partial(kernel, gather, layer), out_shape=(jax.S...]
where the time goes in v3:
time: 51 us; the launch traced here: 50.9 us
  Pallas kernels  50.3 us (99%)
  between operations  0.64 us (1%)
    pallas_call x1, Pallas kernels, on_device(): pl.pallas_call(functools.partial(kernel, gather, layer), out_shape=(jax.S...  46.9 us
    pallas_call x1, Pallas kernels, on_device(): pl.pallas_call(write_out, out_shape=(jax.ShapeDtypeStruct((2, 2, 4, high,...  3.34 us

profile of v3, /device:TPU:1, one launch (start us, length us, event | category | flops | bytes accessed | tf_op | source)
XLA Modules:
  0.0 50.9 jit_solution(16910419086195110143)
XLA Ops:
  0.6 46.9 %shard_map.147 = (bf16[2,2,4,48,4096]{4,3,2,1,0:T(8,128)(2,1)S(1)}, f32[8,8,512]{2,1,0:T(8,128)S(1)}) custom-call(s32[4]{0:T(128)} %refs_0_.1, bf16[2,4,4096]{2,1,0:T(4,128)(2,1)} %refs_1_.1, f32[1,4096]{1,0:T(1,128)} %bitcast.4, bf16[32,4096]{1,0:T(8,128)(2,1)} %refs_3_.1, bf16[8,4096]{1,0:T(8,128)(2,1)} %refs_4_.1, bf16[8,4096]{1,0:T(8,128)(2,1)} %refs_5_.1, ...), custom_call_target="tpu_custom_call" | custom-call | flops 1000000000 | bytes 41943040 | tf_op jit(solution)/shard_map/pallas_call | solution.py:649
  47.6 3.3 %shard_map.148 = (bf16[2,2,4,32,4096]{4,3,2,1,0:T(8,128)(2,1)}, bf16[2,2,32,4096]{3,2,1,0:T(8,128)(2,1)}, bf16[2,2,32,4096]{3,2,1,0:T(8,128)(2,1)}, bf16[2,4,4096]{2,1,0:T(4,128)(2,1)}) custom-call(bf16[2,2,4,48,4096]{4,3,2,1,0:T(8,128)(2,1)S(1)} %get-tuple-element.10.held, f32[8,8,512]{2,1,0:T(8,128)S(1)} %get-tuple-element.11.mixed), custom_call_target="tpu_custom_call" | custom-call | tf_op jit(solution)/shard_map/pallas_call | solution.py:690

commit v4 on v3

--- a/solution.py
+++ b/solution.py
@@ -67,7 +67,7 @@
         self.middle = jnp.logical_not(self.edge)
         self.ends = []
 
-    def greet(self, loads):
+    def greet(self):
         x, y, z, core = self.x, self.y, self.z, self.core
         barrier = pltpu.get_barrier_semaphore()
 
@@ -82,9 +82,11 @@
         signal(row(y, 1) + row(y // 2 * 2 + 1 - y % 2))
         pl.when(self.edge)(lambda: signal([device(x, 3 - y, z, core)]))
         pl.when(self.middle)(lambda: signal(row(y % 2 * 2) + row(y % 2 * 2 + 1)))
+
+    def meet(self, loads):
         for load in loads:
             load.wait()
-        pl.semaphore_wait(barrier, 15 + self.edge.astype(jnp.int32))
+        pl.semaphore_wait(pltpu.get_barrier_semaphore(), 15 + self.edge.astype(jnp.int32))
 
     def send(self, source, target, sent, got, to, when=None):
         copy = pltpu.make_async_remote_copy(
@@ -578,6 +580,7 @@
     sources, (held, mixed) = refs[6:12], refs[12:14]
     moved, ring, late, small, sent, got, own, hidden_here, gain_here, lengths_here = refs[14:24]
     gather.begin(held, moved, ring, late, sent, got)
+    gather.greet()
     high, low = q.shape[0], k.shape[0]
     pairs = [
         (q, moved.at[0, pl.ds(0, high), :]),
@@ -591,7 +594,7 @@
     for load in loads:
         load.start()
     layer.begin(hidden_here, lengths_here, gain_here, sources, mixed, refs[24:])
-    gather.greet(loads)
+    gather.meet(loads)
     moved[0, pl.ds(high, 2 * low), :] = jnp.concatenate([small[0], small[1]], axis=0)
     steps = [*gather.steps().values(), *layer.steps().values()]
     for number in ORDER:

time: 51 us -> 51.6 us (1.012)
    pallas_call x1, Pallas kernels: 46.9 us -> 47.5 us  [on_device(): pl.pallas_call(functools.partial(kernel, gather, layer), out_shape=(jax.S...]
where the time goes in v4:
time: 51.6 us; the launch traced here: 51.4 us
  Pallas kernels  50.8 us (98%)
  between operations  0.64 us (1%)
    pallas_call x1, Pallas kernels, on_device(): pl.pallas_call(functools.partial(kernel, gather, layer), out_shape=(jax.S...  47.5 us
    pallas_call x1, Pallas kernels, on_device(): pl.pallas_call(write_out, out_shape=(jax.ShapeDtypeStruct((2, 2, 4, high,...  3.34 us

profile of v4, /device:TPU:1, one launch (start us, length us, event | category | flops | bytes accessed | tf_op | source)
XLA Modules:
  0.0 51.4 jit_solution(4183780108427936189)
XLA Ops:
  0.6 47.5 %shard_map.147 = (bf16[2,2,4,48,4096]{4,3,2,1,0:T(8,128)(2,1)S(1)}, f32[8,8,512]{2,1,0:T(8,128)S(1)}) custom-call(s32[4]{0:T(128)} %refs_0_.1, bf16[2,4,4096]{2,1,0:T(4,128)(2,1)} %refs_1_.1, f32[1,4096]{1,0:T(1,128)} %bitcast.4, bf16[32,4096]{1,0:T(8,128)(2,1)} %refs_3_.1, bf16[8,4096]{1,0:T(8,128)(2,1)} %refs_4_.1, bf16[8,4096]{1,0:T(8,128)(2,1)} %refs_5_.1, ...), custom_call_target="tpu_custom_call" | custom-call | flops 1000000000 | bytes 41943040 | tf_op jit(solution)/shard_map/pallas_call | solution.py:652
  48.1 3.3 %shard_map.148 = (bf16[2,2,4,32,4096]{4,3,2,1,0:T(8,128)(2,1)}, bf16[2,2,32,4096]{3,2,1,0:T(8,128)(2,1)}, bf16[2,2,32,4096]{3,2,1,0:T(8,128)(2,1)}, bf16[2,4,4096]{2,1,0:T(4,128)(2,1)}) custom-call(bf16[2,2,4,48,4096]{4,3,2,1,0:T(8,128)(2,1)S(1)} %get-tuple-element.10.held, f32[8,8,512]{2,1,0:T(8,128)S(1)} %get-tuple-element.11.mixed), custom_call_target="tpu_custom_call" | custom-call | tf_op jit(solution)/shard_map/pallas_call | solution.py:693
